TPU v7x, 128 devices: a whole 4x4x4 slice. The times are simulated.
128 devices in a mesh: occ: 4 (over y_hi, core), aux: 32 (over x, z, y_lo).
Axes of the slice: x: 4, y: 4 (y_hi: 2, y_lo: 2; y = y_hi * 2 + y_lo), z: 4, core: 2. Of those that a mesh axis runs over, the one named last changes fastest.
Arguments:
- three_index: bfloat16 [12000, 6, 1920], P('aux'), may hold values from -0.47851562 to 0.47851562
- occ_energy: float32 [6], replicated, may hold values from -1.5 to -0.3
- vir_energy: float32 [1920], replicated, may hold values from 0.25 to 2.95
- batch_table: int32 [6], replicated, may hold values from 0 to 5, each once
- orbital_order: int32 [6], replicated, may hold values from 0 to 5, each once
- occ_pair_int: bfloat16 [2, 2, 12000], P(None, None, 'aux'), may hold values from -0.03881836 to 0.03881836
- half_ao: bfloat16 [2, 12000, 4000], P(None, 'aux'), may hold values from -9.536743e-06 to 9.536743e-06
- vir_coeff: bfloat16 [4000, 1920], P('aux', 'occ'), may hold values from -0.09375 to 0.09375
Outputs:
- gamma: bfloat16 [12000, 2, 1920], P('aux', None, 'occ')
- orbital_gradient: float32 [2, 1920], P(None, ('occ', 'aux'))
Inputs may be any that keep to these rules, and one draw needn't show every extreme that they name: `batch_table`: a permutation of 0 to 5; its first 4 entries are the partner orbitals of the window. `orbital_order`: a permutation of 0 to 5; its first 2 entries are the orbitals whose amplitudes are formed.
All inputs are finite; a program needn't handle non-finite values.
Results may differ from a plain program's by a relative error of at most 0.019.
Values may be sent and summed in bfloat16 or wider, within the bound.
No kernel may reach another device: no remote copies, remote signals or barrier semaphores. Data moves between devices by JAX's collectives and lax.ppermute only.
A program may use at most 128 MiB of HBM per device.

v0:
```python
import jax
import jax.numpy as jnp
from jax import lax
from jax.sharding import Mesh
from jax.sharding import PartitionSpec as P

NI = 2
KH = 2
ROWS = 30
PAD = 32
AUX = ("x", "z", "yl")
OCC_AUX = ("yh", "core", "x", "z", "yl")
F32 = jnp.float32
BF16 = jnp.bfloat16


def ring(n, d):
    return [(i, (i + d) % n) for i in range(n)]


def up(v, axis):
    return lax.ppermute(v, axis, ring(4, 1))


def down(v, axis):
    return lax.ppermute(v, axis, ring(4, -1))


def dot(a, b, dims):
    return lax.dot_general(a, b, (dims, ((), ())), preferred_element_type=F32)


def ring_sum(v, axis):
    lo2, hi2 = v[2]
    got_up = up(lo2.astype(BF16), axis)
    got_down = down(hi2.astype(BF16), axis)
    one = jnp.concatenate([v[1][0] + got_up.astype(F32), v[1][1]]).astype(BF16)
    three = jnp.concatenate([v[3][0], v[3][1] + got_down.astype(F32)]).astype(BF16)
    from_below = up(one, axis)
    from_above = down(three, axis)
    own = jnp.concatenate([v[0][0], v[0][1]])
    return own + from_below.astype(F32) + from_above.astype(F32)


def ring_gather(v, axis):
    below = up(v, axis)
    above = down(v, axis)
    half = v.shape[0] // 2
    lo = up(below[:half], axis)
    hi = down(above[half:], axis)
    return [v, above, jnp.concatenate([lo, hi]), below]


def local(
    three_index,
    occ_energy,
    vir_energy,
    batch_table,
    orbital_order,
    occ_pair_int,
    half_ao,
    vir_coeff,
):
    nq, _, nvirt = three_index.shape
    yh, core, x, z, yl = (lax.axis_index(a) for a in OCC_AUX)
    own_a = (yh * 2 + core) * (nvirt // 4)
    by_orbital = jnp.transpose(three_index, (1, 0, 2))

    def orbital(i):
        return lax.dynamic_index_in_dim(by_orbital, i, 0, keepdims=False)

    def partner_orbital(half, k):
        return lax.dynamic_index_in_dim(batch_table, half * KH + k, 0, keepdims=False)

    pairs = []
    for h in range(2):
        for c in range(2):
            for t in range(2):
                src = h * 4 + c * 2 + t
                dst = (h if c == 0 else 1 - h) * 4 + c * 2 + (1 - t)
                pairs.append((src, dst))
    swap = lambda v: lax.ppermute(v, ("yh", "core", "yl"), pairs)
    right_sent = orbital(partner_orbital(1 - yl, core))
    right_first = swap(right_sent)
    right_second = lax.ppermute(right_first, "core", [(0, 1), (1, 0)])
    place = lax.broadcasted_iota(jnp.int32, (16 * PAD, 1), 0)
    dx, dz, r = (place // (4 * PAD), place // PAD % 4, place % PAD)
    chunk = (x + dx) % 4 * 4 + (z + dz) % 4
    virt = jnp.where(r < ROWS, chunk * ROWS + r, -nvirt)

    def left_rows(first):
        hot = (lax.broadcasted_iota(jnp.int32, (1, nvirt), 1) == virt + first).astype(BF16)
        both = [
            dot(hot, orbital(orbital_order[s]), ((1,), (1,))).astype(BF16).reshape(16, 1, PAD, nq)
            for s in range(NI)
        ]
        return jnp.concatenate(both, axis=1).reshape(16 * NI * PAD, nq)

    target_yh = jnp.where(core == 0, yh, 1 - yh)
    left_own = left_rows(own_a)
    left_sent = left_rows((target_yh * 2 + core) * (nvirt // 4))
    left_other = swap(left_sent)
    right_own = [orbital(partner_orbital(yl, k)) for k in range(KH)]
    right_other = [
        jnp.where(core == 0, right_first, right_second),
        jnp.where(core == 0, right_second, right_first),
    ]
    pair_flat = occ_pair_int.reshape(NI * NI, nq)
    g = [dot(pair_flat, half_ao[t], ((1,), (0,))) for t in range(NI)]
    cell = lambda u, v, t: g[t][u * NI + v]
    fock_terms = []
    for s in range(NI):
        fock_terms.append(2.0 * cell(0, 0, s) - cell(s, 0, 0))
        fock_terms.append(2.0 * (cell(0, 1, s) + cell(1, 0, s)) - cell(s, 1, 0) - cell(s, 0, 1))
        fock_terms.append(2.0 * cell(1, 1, s) - cell(s, 1, 1))
    fock_terms = jnp.stack(fock_terms)
    n_aux = lax.axis_size(AUX)
    tile = half_ao.shape[2] // n_aux
    fock_tile = lax.psum_scatter(
        fock_terms.reshape(6, n_aux, tile).transpose(1, 0, 2), AUX, scatter_dimension=0, tiled=False
    )
    vir_part = jnp.dot(fock_tile, vir_coeff.astype(F32), precision=lax.Precision.HIGHEST)
    share = vir_part.shape[1] // n_aux
    vir_own = lax.psum_scatter(
        vir_part.reshape(6, n_aux, share).transpose(1, 0, 2), AUX, scatter_dimension=0, tiled=False
    )
    pair_other = lax.ppermute(pair_flat, "yl", [(0, 1), (1, 0)])
    z_part = jnp.stack(
        [
            dot(pair_flat, right_own[k], ((1,), (0,)))
            + dot(pair_other, right_other[k], ((1,), (0,)))
            for k in range(KH)
        ]
    )
    z_sum = lax.psum(z_part, ("x", "z"))

    def by_block(left, swapped):
        blocks = left.reshape(4, 4, NI * PAD, nq)
        blocks = blocks.transpose(1, 0, 2, 3) if swapped else blocks
        return blocks.reshape(4, 2, 2 * NI * PAD, nq)

    summed = []
    for k, (first, second) in enumerate((("x", "z"), ("z", "x"))):
        lo_, oo_ = (by_block(left_own, k == 1), by_block(left_other, k == 1))
        v = {}
        for d in (2, 1, 3, 0):
            v[d] = [
                dot(lo_[d, h], right_own[k], ((1,), (0,)))
                + dot(oo_[d, h], right_other[k], ((1,), (0,)))
                for h in range(2)
            ]
        u = ring_sum(v, first).reshape(4, 2, PAD, nvirt)
        w = ring_sum([[u[d, 0], u[d, 1]] for d in range(4)], second)
        summed.append(w.reshape(NI, PAD, nvirt))
    own_chunk = x * 4 + z
    padded = jnp.concatenate([vir_energy, vir_energy[:2]])
    row_energy = lax.dynamic_slice_in_dim(padded, own_a + own_chunk * ROWS, PAD)
    left_energy = jnp.stack([occ_energy[orbital_order[s]] for s in range(NI)])
    amps = []
    for k in range(KH):
        e_k = lax.dynamic_index_in_dim(occ_energy, partner_orbital(yl, k), 0, keepdims=False)
        denominator = (
            row_energy[None, :, None] + vir_energy[None, None, :] - left_energy[:, None, None] - e_k
        )
        amps.append((-summed[k] / denominator).astype(BF16))
    wide = [a.astype(F32) for a in amps]
    entries = [-sum((jnp.sum(w[s] * w[t]) for w in wide)) for s, t in ((0, 0), (0, 1), (1, 1))]
    density = lax.psum(jnp.stack(entries), OCC_AUX)
    occ_rows = []
    for s in range(NI):
        row = jnp.zeros((PAD,), F32)
        for k in range(KH):
            for u in range(NI):
                row = row - jnp.sum(wide[k][u] * z_sum[k, u * NI + s][None, :], axis=1)
        occ_rows.append(row)
    occ_rows = jnp.stack(occ_rows)
    mine = lax.dynamic_slice_in_dim(occ_rows, yl * share, share, axis=1)
    theirs = lax.dynamic_slice_in_dim(occ_rows, (1 - yl) * share, share, axis=1)
    occ_side = mine + lax.ppermute(theirs, "yl", [(0, 1), (1, 0)])
    gammas = []
    for k, (first, second) in enumerate((("z", "x"), ("x", "z"))):
        own = jnp.concatenate(ring_gather(amps[k].reshape(NI * PAD, nvirt), first))
        blocks = ring_gather(own, second)
        parts = [
            [dot(b, right[k], ((1,), (1,))) for b in blocks] for right in (right_other, right_own)
        ]
        both = [jnp.concatenate(p).reshape(4, 4, NI * PAD, nq) for p in parts]
        if k == 1:
            both = [b.transpose(1, 0, 2, 3) for b in both]
        gammas.append(both)
    gamma_sent = (gammas[0][0] + gammas[1][0]).astype(BF16)
    gamma_got = lax.ppermute(gamma_sent, "yl", [(0, 1), (1, 0)])
    gamma_rows = (gammas[0][1] + gammas[1][1] + gamma_got.astype(F32)).astype(BF16)
    gamma_rows = gamma_rows.reshape(16, NI, PAD, nq)
    target = lax.broadcasted_iota(jnp.int32, (nvirt // 4, 1), 0)
    back = (target == virt.reshape(1, 16 * PAD)).astype(BF16)
    gamma_out = jnp.stack(
        [
            dot(back, gamma_rows[:, s].reshape(16 * PAD, nq), ((1,), (0,))).astype(BF16)
            for s in range(NI)
        ]
    )
    gamma_out = jnp.transpose(gamma_out, (2, 0, 1))
    weights = vir_own.reshape(NI, 3, share)
    gradient = occ_side + jnp.sum(weights * density[None, :, None], axis=1)
    return (gamma_out, gradient)


def solution(mesh):
    torus = Mesh(mesh.devices.reshape(2, 2, 4, 4, 2), OCC_AUX)
    occ = ("yh", "core")
    return jax.shard_map(
        local,
        mesh=torus,
        in_specs=(
            P(AUX, None, None),
            P(),
            P(),
            P(),
            P(),
            P(None, None, AUX),
            P(None, AUX, None),
            P(AUX, occ),
        ),
        out_specs=(P(AUX, None, occ), P(None, OCC_AUX)),
        check_vma=False,
    )
```

profile of v0, /device:TPU:0, one launch (start us, length us, event | category | flops | bytes accessed | tf_op | source)
XLA Modules:
  0.0 838.8 jit_solution(4391718574668692102)
XLA Ops:
  28.3 13.4 %fusion.165 = (bf16[1,375,4000]{2,0,1:T(2,128)(2,1)}, bf16[1,375,4000]{2,0,1:T(2,128)(2,1)}) fusion(bf16[2,375,4000]{2,0,1:T(2,128)(2,1)} %param.14), kind=kLoop, calls=%fused_computation.334 | loop fusion | bytes 12000000 | tf_op jit(solution)/shard_map/slice | solution.py:109
  41.7 13.8 %copy.135 = bf16[1,375,4000]{1,2,0:T(8,128)(2,1)S(1)} copy(bf16[1,375,4000]{2,0,1:T(2,128)(2,1)} %get-tuple-element.35) | data formatting | bytes 6000000
  56.4 13.9 %copy.134 = bf16[1,375,4000]{1,2,0:T(8,128)(2,1)S(1)} copy(bf16[1,375,4000]{2,0,1:T(2,128)(2,1)} %get-tuple-element.34) | data formatting | bytes 6000000
  111.6 2.8 fusion.51
  133.1 221.0 %all-reduce.4.cloned.1.call-done = f32[32,6,125]{2,1,0:T(8,128)} async-done(((f32[32,6,125]{2,1,0:T(8,128)}), f32[32,6,125]{2,1,0:T(8,128)}) %all-reduce.4.cloned.1.call-update) | async-done | bytes 96016
  356.1 154.6 %all-reduce.1 = f32[32,6,15]{2,1,0:T(8,128)S(1)} all-reduce(f32[32,6,15]{2,1,0:T(8,128)S(1)} %copy.133), channel_id=3, replica_groups=mesh['yh'=2,'core'=2,'x'=4,'z'=4,'yl'=2] {'x','z','yl'}, use_global_device_ids=true, to_apply=%region_10.11.clone | all-reduce | flops 2880 | bytes 23040
  519.9 3.2 collective-permute-start.5
  530.9 3.2 collective-permute-start.21
  537.5 70.3 %psum.14 = f32[2,4,1920]{2,1,0:T(4,128)S(1)} all-reduce(f32[2,4,1920]{2,1,0:T(4,128)S(1)} %pad_maximum_fusion.14), channel_id=1, replica_groups=mesh['yh'=2,'core'=2,'x'=4,'z'=4,'yl'=2] {'x','z'}, use_global_device_ids=true, to_apply=%region_0.1 | all-reduce | flops 15360 | bytes 122880 | tf_op jit(solution)/shard_map/psum | solution.py:135
  623.5 3.2 collective-permute-done.4
  628.8 3.2 collective-permute-start.9
  635.7 3.2 collective-permute-start.25
  639.1 3.8 collective-permute-start.10
  643.1 3.3 collective-permute-start.26
  646.9 3.5 collective-permute-done.24
  654.3 3.3 collective-permute-start.27
  668.1 65.9 %psum.15 = f32[3]{0:T(128)S(1)} all-reduce(f32[3]{0:T(128)S(1)} %pad_maximum_fusion.17), channel_id=1, replica_groups=mesh['yh'=2,'core'=2,'x'=4,'z'=4,'yl'=2] {'yh','core','x','z','yl'}, use_global_device_ids=true, to_apply=%region_17.18 | all-reduce | flops 3 | bytes 24 | tf_op jit(solution)/shard_map/psum | solution.py:168
  761.0 3.1 fusion.43
  764.1 2.9 fusion.69
  768.2 7.1 collective-permute-done.32
  775.6 3.3 collective-permute-start.34
  782.7 3.2 collective-permute-start.18
  805.9 3.0 copy.121
  821.3 6.9 collective-permute-done.35
  (322 shorter events, 195.0 us)
Async XLA Ops:
  7.2 347.0 %all-reduce.4.cloned.1.call-start = ((), (), s32[]{:S(2)}) async-start(), calls=%async_computation | async-start | bytes 262144
  13.1 112.5 %collective-permute-start.1 = (bf16[375,1920]{1,0:T(8,128)(2,1)}, bf16[375,1920]{1,0:T(8,128)(2,1)}, u32[]{:S(2)}, u32[]{:S(2)}) collective-permute-start(bf16[375,1920]{1,0:T(8,128)(2,1)} %dynamic-slice_bitcast_fusion), channel_id=1, source_target_pairs={{0,1},{1,0},{32,97},{33,96},{64,65},{65,64},{96,33},{97,32},{2,3},... | collective-permute-start | bytes 4320008 | tf_op jit(solution)/shard_map/ppermute | solution.py:82
  26.0 485.3 %collective-permute-start = (bf16[1024,375]{0,1:T(8,128)(2,1)}, bf16[1024,375]{0,1:T(8,128)(2,1)}, u32[]{:S(2)}, u32[]{:S(2)}) collective-permute-start(bf16[1024,375]{0,1:T(8,128)(2,1)} %copy.104), channel_id=1, source_target_pairs={{0,1},{1,0},{32,97},{33,96},{64,65},{65,64},{96,33},{97,32},{2,3},... | collective-permute-start | bytes 2304008 | tf_op jit(solution)/shard_map/ppermute | solution.py:82
  26.4 510.5 %collective-permute-start.36 = (bf16[4,375]{1,0:T(4,128)(2,1)S(1)}, bf16[4,375]{1,0:T(4,128)(2,1)S(1)}, u32[]{:S(2)}, u32[]{:S(2)}) collective-permute-start(bf16[4,375]{1,0:T(4,128)(2,1)S(1)} %reshape.436), channel_id=1, source_target_pairs={{0,1},{1,0},{2,3},{3,2},{4,5},{5,4},{6,7},{7,6},{8,9},{9,8},{10,11... | collective-permute-start | bytes 9008 | tf_op jit(solution)/shard_map/ppermute | solution.py:127
  125.6 388.0 %collective-permute-start.2 = (bf16[375,1920]{1,0:T(8,128)(2,1)}, bf16[375,1920]{1,0:T(8,128)(2,1)}, u32[]{:S(2)}, u32[]{:S(2)}) collective-permute-start(bf16[375,1920]{1,0:T(8,128)(2,1)} %collective-permute-done.1), channel_id=1, source_target_pairs={{0,32},{32,0},{1,33},{33,1},{2,34},{34,2},{3,35},{35,3},{4,36},{36... | collective-permute-start | bytes 4320008 | tf_op jit(solution)/shard_map/ppermute | solution.py:85
  517.5 92.3 %collective-permute-start.3 = (bf16[128,1920]{1,0:T(8,128)(2,1)}, bf16[128,1920]{1,0:T(8,128)(2,1)}, u32[]{:S(2)}, u32[]{:S(2)}) collective-permute-start(bf16[128,1920]{1,0:T(8,128)(2,1)} %fusion.13), channel_id=1, source_target_pairs={{0,8},{8,16},{16,24},{24,0},{1,9},{9,17},{17,25},{25,1},{2,10},{10... | collective-permute-start | bytes 1474568 | tf_op jit(solution)/shard_map/ppermute | solution.py:22
  519.9 91.6 %collective-permute-start.5 = (bf16[128,1920]{1,0:T(8,128)(2,1)}, bf16[128,1920]{1,0:T(8,128)(2,1)}, u32[]{:S(2)}, u32[]{:S(2)}) collective-permute-start(bf16[128,1920]{1,0:T(8,128)(2,1)} %fusion.17), channel_id=1, source_target_pairs={{0,24},{8,0},{16,8},{24,16},{1,25},{9,1},{17,9},{25,17},{2,26},{10... | collective-permute-start | bytes 1474568 | tf_op jit(solution)/shard_map/ppermute | solution.py:26
  528.4 88.1 %collective-permute-start.19 = (bf16[128,1920]{1,0:T(8,128)(2,1)}, bf16[128,1920]{1,0:T(8,128)(2,1)}, u32[]{:S(2)}, u32[]{:S(2)}) collective-permute-start(bf16[128,1920]{1,0:T(8,128)(2,1)} %fusion.19), channel_id=1, source_target_pairs={{0,2},{2,4},{4,6},{6,0},{1,3},{3,5},{5,7},{7,1},{8,10},{10,12},{12... | collective-permute-start | bytes 1474568 | tf_op jit(solution)/shard_map/ppermute | solution.py:22
  530.9 87.7 %collective-permute-start.21 = (bf16[128,1920]{1,0:T(8,128)(2,1)}, bf16[128,1920]{1,0:T(8,128)(2,1)}, u32[]{:S(2)}, u32[]{:S(2)}) collective-permute-start(bf16[128,1920]{1,0:T(8,128)(2,1)} %fusion.23), channel_id=1, source_target_pairs={{0,6},{2,0},{4,2},{6,4},{1,7},{3,1},{5,3},{7,5},{8,14},{10,8},{12,... | collective-permute-start | bytes 1474568 | tf_op jit(solution)/shard_map/ppermute | solution.py:26
  618.1 15.8 %collective-permute-start.20 = (bf16[256,1920]{1,0:T(8,128)(2,1)S(1)}, bf16[256,1920]{1,0:T(8,128)(2,1)S(1)}, u32[]{:S(2)}, u32[]{:S(2)}) collective-permute-start(bf16[256,1920]{1,0:T(8,128)(2,1)S(1)} %pad_maximum_fusion.6), channel_id=1, source_target_pairs={{0,2},{2,4},{4,6},{6,0},{1,3},{3,5},{5,7},{7,1},{8,10},{10,12},{12... | collective-permute-start | bytes 2949128 | tf_op jit(solution)/shard_map/ppermute | solution.py:22
  654.3 83.3 %collective-permute-start.27 = (bf16[64,1920]{1,0:T(8,128)(2,1)}, bf16[64,1920]{1,0:T(8,128)(2,1)}, u32[]{:S(2)}, u32[]{:S(2)}) collective-permute-start(bf16[64,1920]{1,0:T(8,128)(2,1)} %get-tuple-element.30), channel_id=1, source_target_pairs={{0,24},{8,0},{16,8},{24,16},{1,25},{9,1},{17,9},{25,17},{2,26},{10... | collective-permute-start | bytes 737288 | tf_op jit(solution)/shard_map/ppermute | solution.py:26
  657.7 77.1 %collective-permute-start.28 = (bf16[64,1920]{1,0:T(8,128)(2,1)}, bf16[64,1920]{1,0:T(8,128)(2,1)}, u32[]{:S(2)}, u32[]{:S(2)}) collective-permute-start(bf16[64,1920]{1,0:T(8,128)(2,1)} %get-tuple-element.30), channel_id=1, source_target_pairs={{0,8},{8,16},{16,24},{24,0},{1,9},{9,17},{17,25},{25,1},{2,10},{10... | collective-permute-start | bytes 737288 | tf_op jit(solution)/shard_map/ppermute | solution.py:22
  658.4 84.4 %collective-permute-start.11 = (bf16[64,1920]{1,0:T(8,128)(2,1)S(1)}, bf16[64,1920]{1,0:T(8,128)(2,1)}, u32[]{:S(2)}, u32[]{:S(2)}) collective-permute-start(bf16[64,1920]{1,0:T(8,128)(2,1)S(1)} %get-tuple-element.58), channel_id=1, source_target_pairs={{0,6},{2,0},{4,2},{6,4},{1,7},{3,1},{5,3},{7,5},{8,14},{10,8},{12,... | collective-permute-start | bytes 737288 | tf_op jit(solution)/shard_map/ppermute | solution.py:26
  661.0 79.0 %collective-permute-start.12 = (bf16[64,1920]{1,0:T(8,128)(2,1)S(1)}, bf16[64,1920]{1,0:T(8,128)(2,1)}, u32[]{:S(2)}, u32[]{:S(2)}) collective-permute-start(bf16[64,1920]{1,0:T(8,128)(2,1)S(1)} %get-tuple-element.58), channel_id=1, source_target_pairs={{0,2},{2,4},{4,6},{6,0},{1,3},{3,5},{5,7},{7,1},{8,10},{10,12},{12... | collective-permute-start | bytes 737288 | tf_op jit(solution)/shard_map/ppermute | solution.py:22
  668.1 66.0 %collective-permute-start.37 = (f32[2,15]{1,0:T(2,128)S(1)}, f32[2,15]{1,0:T(2,128)S(1)}, u32[]{:S(2)}, u32[]{:S(2)}) collective-permute-start(f32[2,15]{1,0:T(2,128)S(1)} %constant_dynamic-slice_fusion), channel_id=1, source_target_pairs={{0,1},{1,0},{2,3},{3,2},{4,5},{5,4},{6,7},{7,6},{8,9},{9,8},{10,11... | collective-permute-start | bytes 368 | tf_op jit(solution)/shard_map/ppermute | solution.py:179
  751.4 23.9 %collective-permute-start.32 = (bf16[256,1920]{1,0:T(8,128)(2,1)}, bf16[256,1920]{1,0:T(8,128)(2,1)S(1)}, u32[]{:S(2)}, u32[]{:S(2)}) collective-permute-start(bf16[256,1920]{1,0:T(8,128)(2,1)} %constant_dynamic-update-slice_fusion.7), channel_id=1, source_target_pairs={{0,2},{2,4},{4,6},{6,0},{1,3},{3,5},{5,7},{7,1},{8,10},{10,12},{12... | collective-permute-start | bytes 2949128 | tf_op jit(solution)/shard_map/ppermute | solution.py:22
  752.1 23.4 %collective-permute-start.31 = (bf16[256,1920]{1,0:T(8,128)(2,1)}, bf16[256,1920]{1,0:T(8,128)(2,1)S(1)}, u32[]{:S(2)}, u32[]{:S(2)}) collective-permute-start(bf16[256,1920]{1,0:T(8,128)(2,1)} %constant_dynamic-update-slice_fusion.7), channel_id=1, source_target_pairs={{0,6},{2,0},{4,2},{6,4},{1,7},{3,1},{5,3},{7,5},{8,14},{10,8},{12,... | collective-permute-start | bytes 2949128 | tf_op jit(solution)/shard_map/ppermute | solution.py:26
  757.6 23.4 %collective-permute-start.16 = (bf16[256,1920]{1,0:T(8,128)(2,1)}, bf16[256,1920]{1,0:T(8,128)(2,1)S(1)}, u32[]{:S(2)}, u32[]{:S(2)}) collective-permute-start(bf16[256,1920]{1,0:T(8,128)(2,1)} %constant_dynamic-update-slice_fusion), channel_id=1, source_target_pairs={{0,8},{8,16},{16,24},{24,0},{1,9},{9,17},{17,25},{25,1},{2,10},{10... | collective-permute-start | bytes 2949128 | tf_op jit(solution)/shard_map/ppermute | solution.py:22
  758.3 23.5 %collective-permute-start.15 = (bf16[256,1920]{1,0:T(8,128)(2,1)}, bf16[256,1920]{1,0:T(8,128)(2,1)S(1)}, u32[]{:S(2)}, u32[]{:S(2)}) collective-permute-start(bf16[256,1920]{1,0:T(8,128)(2,1)} %constant_dynamic-update-slice_fusion), channel_id=1, source_target_pairs={{0,24},{8,0},{16,8},{24,16},{1,25},{9,1},{17,9},{25,17},{2,26},{10... | collective-permute-start | bytes 2949128 | tf_op jit(solution)/shard_map/ppermute | solution.py:26
  775.4 20.0 %collective-permute-start.33 = (bf16[128,1920]{1,0:T(8,128)(2,1)S(1)}, bf16[128,1920]{1,0:T(8,128)(2,1)S(1)}, u32[]{:S(2)}, u32[]{:S(2)}) collective-permute-start(bf16[128,1920]{1,0:T(8,128)(2,1)S(1)} %slice.422), channel_id=1, source_target_pairs={{0,2},{2,4},{4,6},{6,0},{1,3},{3,5},{5,7},{7,1},{8,10},{10,12},{12... | collective-permute-start | bytes 1474568 | tf_op jit(solution)/shard_map/ppermute | solution.py:22
  775.6 19.9 %collective-permute-start.34 = (bf16[128,1920]{1,0:T(8,128)(2,1)S(1)}, bf16[128,1920]{1,0:T(8,128)(2,1)S(1)}, u32[]{:S(2)}, u32[]{:S(2)}) collective-permute-start(bf16[128,1920]{1,0:T(8,128)(2,1)S(1)} %slice.423), channel_id=1, source_target_pairs={{0,6},{2,0},{4,2},{6,4},{1,7},{3,1},{5,3},{7,5},{8,14},{10,8},{12,... | collective-permute-start | bytes 1474568 | tf_op jit(solution)/shard_map/ppermute | solution.py:26
  781.8 18.4 %collective-permute-start.17 = (bf16[128,1920]{1,0:T(8,128)(2,1)}, bf16[128,1920]{1,0:T(8,128)(2,1)}, u32[]{:S(2)}, u32[]{:S(2)}) collective-permute-start(bf16[128,1920]{1,0:T(8,128)(2,1)} %slice.394), channel_id=1, source_target_pairs={{0,8},{8,16},{16,24},{24,0},{1,9},{9,17},{17,25},{25,1},{2,10},{10... | collective-permute-start | bytes 1474568 | tf_op jit(solution)/shard_map/ppermute | solution.py:22
  782.7 18.7 %collective-permute-start.18 = (bf16[128,1920]{1,0:T(8,128)(2,1)}, bf16[128,1920]{1,0:T(8,128)(2,1)}, u32[]{:S(2)}, u32[]{:S(2)}) collective-permute-start(bf16[128,1920]{1,0:T(8,128)(2,1)} %slice.395), channel_id=1, source_target_pairs={{0,24},{8,0},{16,8},{24,16},{1,25},{9,1},{17,9},{25,17},{2,26},{10... | collective-permute-start | bytes 1474568 | tf_op jit(solution)/shard_map/ppermute | solution.py:26
  811.5 16.8 %collective-permute-start.35 = (bf16[4,4,64,375]{3,2,1,0:T(8,128)(2,1)}, bf16[4,4,64,375]{3,2,1,0:T(8,128)(2,1)}, u32[]{:S(2)}, u32[]{:S(2)}) collective-permute-start(bf16[4,4,64,375]{3,2,1,0:T(8,128)(2,1)} %fusion.32), channel_id=1, source_target_pairs={{0,1},{1,0},{2,3},{3,2},{4,5},{5,4},{6,7},{7,6},{8,9},{9,8},{10,11... | collective-permute-start | bytes 2304008 | tf_op jit(solution)/shard_map/ppermute | solution.py:192
  (63 other events, 370.4 us)
Sparse Core Ops, SparseCore 0:
  73.1 280.9 all-reduce.3
where the time goes:
time: 845 us; the launch traced here: 839 us
  blocking collectives  291 us (34%)
  waiting for transfers between devices  249 us (29%)
  matrix products  107 us (13%)
  local copies, waits for them, and re-layouts  85.2 us (10%)
  starting transfers between devices  57.4 us (7%)
  between operations  28.5 us (3%)
  other arithmetic  21.1 us (2%)
    unnamed x2, waiting for transfers between devices  221 us
    unnamed x1, blocking collectives  155 us
    dot_general x60, matrix products, dot(): return lax.dot_general(a, b, (dims, ((), ())), preferred_element_type=F32)  105 us
    psum x1, blocking collectives, local(): z_sum = lax.psum(z_part, ('x', 'z'))  70.3 us
    psum x1, blocking collectives, local(): density = lax.psum(jnp.stack(entries), OCC_AUX)  65.9 us
    ppermute x16, starting transfers between devices, down(): return lax.ppermute(v, axis, ring(4, -1))  45.5 us
    unnamed x108, local copies, waits for them, and re-layouts  43.4 us
    ppermute x16, waiting for transfers between devices, up(): return lax.ppermute(v, axis, ring(4, 1))  18.4 us
  transfers between devices with their start and end apart: 39, of which 10 were waited for; matrix products, arithmetic and copies ran while one was open for 22% of the time, Pallas kernels for 0%

commit v1 on v0

--- a/solution.py
+++ b/solution.py
@@ -132,7 +132,7 @@
             for k in range(KH)
         ]
     )
-    z_sum = lax.psum(z_part, ("x", "z"))
+    z_sum = lax.psum(lax.psum(z_part, "x"), "z")
 
     def by_block(left, swapped):
         blocks = left.reshape(4, 4, NI * PAD, nq)

time: 845 us -> 805 us (0.953)
  blocking collectives: 291 us -> 250 us
    psum x1 -> x2, blocking collectives: 70.3 us -> 30.1 us  [local(): z_sum = lax.psum(lax.psum(z_part, 'x'), 'z')]
  transfers between devices with their start and end apart: 39 -> 39, of which waited for: 10 -> 10; matrix products, arithmetic and copies ran while one was open for 22% -> 24% of each run, Pallas kernels for 0% -> 0%
where the time goes in v1:
time: 805 us; the launch traced here: 799 us
  blocking collectives  250 us (31%)
  waiting for transfers between devices  249 us (31%)
  matrix products  107 us (13%)
  local copies, waits for them, and re-layouts  84.5 us (10%)
  starting transfers between devices  58.3 us (7%)
  between operations  29 us (4%)
  other arithmetic  21.3 us (3%)
    unnamed x2, waiting for transfers between devices  221 us
    unnamed x1, blocking collectives  155 us
    dot_general x60, matrix products, dot(): return lax.dot_general(a, b, (dims, ((), ())), preferred_element_type=F32)  105 us
    psum x1, blocking collectives, local(): density = lax.psum(jnp.stack(entries), OCC_AUX)  65.5 us
    ppermute x16, starting transfers between devices, down(): return lax.ppermute(v, axis, ring(4, -1))  44.7 us
    unnamed x108, local copies, waits for them, and re-layouts  42.7 us
    psum x2, blocking collectives, local(): z_sum = lax.psum(lax.psum(z_part, 'x'), 'z')  30.1 us
    ppermute x16, waiting for transfers between devices, up(): return lax.ppermute(v, axis, ring(4, 1))  19.2 us
  transfers between devices with their start and end apart: 39, of which 10 were waited for; matrix products, arithmetic and copies ran while one was open for 24% of the time, Pallas kernels for 0%

profile of v1, /device:TPU:0, one launch (start us, length us, event | category | flops | bytes accessed | tf_op | source)
XLA Modules:
  0.0 798.9 jit_solution(13886760663906269118)
XLA Ops:
  28.6 13.4 %fusion.165 = (bf16[1,375,4000]{2,0,1:T(2,128)(2,1)}, bf16[1,375,4000]{2,0,1:T(2,128)(2,1)}) fusion(bf16[2,375,4000]{2,0,1:T(2,128)(2,1)} %param.14), kind=kLoop, calls=%fused_computation.334 | loop fusion | bytes 12000000 | tf_op jit(solution)/shard_map/slice | solution.py:109
  42.0 13.8 %copy.135 = bf16[1,375,4000]{1,2,0:T(8,128)(2,1)S(1)} copy(bf16[1,375,4000]{2,0,1:T(2,128)(2,1)} %get-tuple-element.35) | data formatting | bytes 6000000
  56.8 13.9 %copy.134 = bf16[1,375,4000]{1,2,0:T(8,128)(2,1)S(1)} copy(bf16[1,375,4000]{2,0,1:T(2,128)(2,1)} %get-tuple-element.34) | data formatting | bytes 6000000
  112.4 2.8 fusion.51
  134.0 220.5 %all-reduce.4.cloned.1.call-done = f32[32,6,125]{2,1,0:T(8,128)} async-done(((f32[32,6,125]{2,1,0:T(8,128)}), f32[32,6,125]{2,1,0:T(8,128)}) %all-reduce.4.cloned.1.call-update) | async-done | bytes 96016
  356.5 154.6 %all-reduce.1 = f32[32,6,15]{2,1,0:T(8,128)S(1)} all-reduce(f32[32,6,15]{2,1,0:T(8,128)S(1)} %copy.133), channel_id=3, replica_groups=mesh['yh'=2,'core'=2,'x'=4,'z'=4,'yl'=2] {'x','z','yl'}, use_global_device_ids=true, to_apply=%region_11.12.clone | all-reduce | flops 2880 | bytes 23040
  520.4 3.2 collective-permute-start.5
  531.4 3.2 collective-permute-start.21
  537.9 15.0 %psum.21 = f32[2,4,1920]{2,1,0:T(4,128)S(1)} all-reduce(f32[2,4,1920]{2,1,0:T(4,128)S(1)} %pad_maximum_fusion.14), channel_id=1, replica_groups=mesh['yh'=2,'core'=2,'x'=4,'z'=4,'yl'=2] {'x'}, use_global_device_ids=true, to_apply=%region_0.1 | all-reduce | flops 15360 | bytes 122880 | tf_op jit(solution)/shard_map/psum | solution.py:135
  553.0 15.1 %psum.22 = f32[2,4,1920]{2,1,0:T(4,128)S(1)} all-reduce(f32[2,4,1920]{2,1,0:T(4,128)S(1)} %psum.21), channel_id=1, replica_groups=mesh['yh'=2,'core'=2,'x'=4,'z'=4,'yl'=2] {'z'}, use_global_device_ids=true, to_apply=%region_1.2 | all-reduce | flops 15360 | bytes 122880 | tf_op jit(solution)/shard_map/psum | solution.py:135
  583.9 3.9 collective-permute-done.4
  596.0 3.2 collective-permute-start.25
  600.1 3.1 collective-permute-start.10
  603.4 3.3 collective-permute-start.26
  607.3 3.5 collective-permute-done.24
  614.8 3.3 collective-permute-start.27
  628.5 65.5 %psum.23 = f32[3]{0:T(128)S(1)} all-reduce(f32[3]{0:T(128)S(1)} %pad_maximum_fusion.17), channel_id=1, replica_groups=mesh['yh'=2,'core'=2,'x'=4,'z'=4,'yl'=2] {'yh','core','x','z','yl'}, use_global_device_ids=true, to_apply=%region_18.19 | all-reduce | flops 3 | bytes 24 | tf_op jit(solution)/shard_map/psum | solution.py:168
  721.1 3.1 fusion.43
  724.2 2.9 fusion.69
  728.3 7.1 collective-permute-done.32
  735.6 3.3 collective-permute-start.34
  742.9 3.2 collective-permute-start.18
  766.1 3.0 copy.121
  781.5 6.9 collective-permute-done.35
  (323 shorter events, 198.9 us)
Async XLA Ops:
  7.2 347.3 %all-reduce.4.cloned.1.call-start = ((), (), s32[]{:S(2)}) async-start(), calls=%async_computation | async-start | bytes 262144
  13.2 113.1 %collective-permute-start.1 = (bf16[375,1920]{1,0:T(8,128)(2,1)}, bf16[375,1920]{1,0:T(8,128)(2,1)}, u32[]{:S(2)}, u32[]{:S(2)}) collective-permute-start(bf16[375,1920]{1,0:T(8,128)(2,1)} %dynamic-slice_bitcast_fusion), channel_id=1, source_target_pairs={{0,1},{1,0},{32,97},{33,96},{64,65},{65,64},{96,33},{97,32},{2,3},... | collective-permute-start | bytes 4320008 | tf_op jit(solution)/shard_map/ppermute | solution.py:82
  26.3 485.4 %collective-permute-start = (bf16[1024,375]{0,1:T(8,128)(2,1)}, bf16[1024,375]{0,1:T(8,128)(2,1)}, u32[]{:S(2)}, u32[]{:S(2)}) collective-permute-start(bf16[1024,375]{0,1:T(8,128)(2,1)} %copy.104), channel_id=1, source_target_pairs={{0,1},{1,0},{32,97},{33,96},{64,65},{65,64},{96,33},{97,32},{2,3},... | collective-permute-start | bytes 2304008 | tf_op jit(solution)/shard_map/ppermute | solution.py:82
  26.7 510.6 %collective-permute-start.36 = (bf16[4,375]{1,0:T(4,128)(2,1)S(1)}, bf16[4,375]{1,0:T(4,128)(2,1)S(1)}, u32[]{:S(2)}, u32[]{:S(2)}) collective-permute-start(bf16[4,375]{1,0:T(4,128)(2,1)S(1)} %reshape.436), channel_id=1, source_target_pairs={{0,1},{1,0},{2,3},{3,2},{4,5},{5,4},{6,7},{7,6},{8,9},{9,8},{10,11... | collective-permute-start | bytes 9008 | tf_op jit(solution)/shard_map/ppermute | solution.py:127
  126.3 387.9 %collective-permute-start.2 = (bf16[375,1920]{1,0:T(8,128)(2,1)}, bf16[375,1920]{1,0:T(8,128)(2,1)}, u32[]{:S(2)}, u32[]{:S(2)}) collective-permute-start(bf16[375,1920]{1,0:T(8,128)(2,1)} %collective-permute-done.1), channel_id=1, source_target_pairs={{0,32},{32,0},{1,33},{33,1},{2,34},{34,2},{3,35},{35,3},{4,36},{36... | collective-permute-start | bytes 4320008 | tf_op jit(solution)/shard_map/ppermute | solution.py:85
  518.0 52.1 %collective-permute-start.3 = (bf16[128,1920]{1,0:T(8,128)(2,1)}, bf16[128,1920]{1,0:T(8,128)(2,1)}, u32[]{:S(2)}, u32[]{:S(2)}) collective-permute-start(bf16[128,1920]{1,0:T(8,128)(2,1)} %fusion.13), channel_id=1, source_target_pairs={{0,8},{8,16},{16,24},{24,0},{1,9},{9,17},{17,25},{25,1},{2,10},{10... | collective-permute-start | bytes 1474568 | tf_op jit(solution)/shard_map/ppermute | solution.py:22
  520.4 51.8 %collective-permute-start.5 = (bf16[128,1920]{1,0:T(8,128)(2,1)}, bf16[128,1920]{1,0:T(8,128)(2,1)}, u32[]{:S(2)}, u32[]{:S(2)}) collective-permute-start(bf16[128,1920]{1,0:T(8,128)(2,1)} %fusion.17), channel_id=1, source_target_pairs={{0,24},{8,0},{16,8},{24,16},{1,25},{9,1},{17,9},{25,17},{2,26},{10... | collective-permute-start | bytes 1474568 | tf_op jit(solution)/shard_map/ppermute | solution.py:26
  528.9 47.9 %collective-permute-start.19 = (bf16[128,1920]{1,0:T(8,128)(2,1)}, bf16[128,1920]{1,0:T(8,128)(2,1)}, u32[]{:S(2)}, u32[]{:S(2)}) collective-permute-start(bf16[128,1920]{1,0:T(8,128)(2,1)} %fusion.19), channel_id=1, source_target_pairs={{0,2},{2,4},{4,6},{6,0},{1,3},{3,5},{5,7},{7,1},{8,10},{10,12},{12... | collective-permute-start | bytes 1474568 | tf_op jit(solution)/shard_map/ppermute | solution.py:22
  531.4 48.2 %collective-permute-start.21 = (bf16[128,1920]{1,0:T(8,128)(2,1)}, bf16[128,1920]{1,0:T(8,128)(2,1)}, u32[]{:S(2)}, u32[]{:S(2)}) collective-permute-start(bf16[128,1920]{1,0:T(8,128)(2,1)} %fusion.23), channel_id=1, source_target_pairs={{0,6},{2,0},{4,2},{6,4},{1,7},{3,1},{5,3},{7,5},{8,14},{10,8},{12,... | collective-permute-start | bytes 1474568 | tf_op jit(solution)/shard_map/ppermute | solution.py:26
  571.8 16.1 %collective-permute-start.4 = (bf16[256,1920]{1,0:T(8,128)(2,1)S(1)}, bf16[256,1920]{1,0:T(8,128)(2,1)S(1)}, u32[]{:S(2)}, u32[]{:S(2)}) collective-permute-start(bf16[256,1920]{1,0:T(8,128)(2,1)S(1)} %pad_maximum_fusion.4), channel_id=1, source_target_pairs={{0,8},{8,16},{16,24},{24,0},{1,9},{9,17},{17,25},{25,1},{2,10},{10... | collective-permute-start | bytes 2949128 | tf_op jit(solution)/shard_map/ppermute | solution.py:22
  614.8 82.8 %collective-permute-start.27 = (bf16[64,1920]{1,0:T(8,128)(2,1)}, bf16[64,1920]{1,0:T(8,128)(2,1)}, u32[]{:S(2)}, u32[]{:S(2)}) collective-permute-start(bf16[64,1920]{1,0:T(8,128)(2,1)} %get-tuple-element.30), channel_id=1, source_target_pairs={{0,24},{8,0},{16,8},{24,16},{1,25},{9,1},{17,9},{25,17},{2,26},{10... | collective-permute-start | bytes 737288 | tf_op jit(solution)/shard_map/ppermute | solution.py:26
  618.1 76.7 %collective-permute-start.28 = (bf16[64,1920]{1,0:T(8,128)(2,1)}, bf16[64,1920]{1,0:T(8,128)(2,1)}, u32[]{:S(2)}, u32[]{:S(2)}) collective-permute-start(bf16[64,1920]{1,0:T(8,128)(2,1)} %get-tuple-element.30), channel_id=1, source_target_pairs={{0,8},{8,16},{16,24},{24,0},{1,9},{9,17},{17,25},{25,1},{2,10},{10... | collective-permute-start | bytes 737288 | tf_op jit(solution)/shard_map/ppermute | solution.py:22
  618.8 83.9 %collective-permute-start.11 = (bf16[64,1920]{1,0:T(8,128)(2,1)S(1)}, bf16[64,1920]{1,0:T(8,128)(2,1)}, u32[]{:S(2)}, u32[]{:S(2)}) collective-permute-start(bf16[64,1920]{1,0:T(8,128)(2,1)S(1)} %get-tuple-element.58), channel_id=1, source_target_pairs={{0,6},{2,0},{4,2},{6,4},{1,7},{3,1},{5,3},{7,5},{8,14},{10,8},{12,... | collective-permute-start | bytes 737288 | tf_op jit(solution)/shard_map/ppermute | solution.py:26
  621.4 78.6 %collective-permute-start.12 = (bf16[64,1920]{1,0:T(8,128)(2,1)S(1)}, bf16[64,1920]{1,0:T(8,128)(2,1)}, u32[]{:S(2)}, u32[]{:S(2)}) collective-permute-start(bf16[64,1920]{1,0:T(8,128)(2,1)S(1)} %get-tuple-element.58), channel_id=1, source_target_pairs={{0,2},{2,4},{4,6},{6,0},{1,3},{3,5},{5,7},{7,1},{8,10},{10,12},{12... | collective-permute-start | bytes 737288 | tf_op jit(solution)/shard_map/ppermute | solution.py:22
  628.5 65.7 %collective-permute-start.37 = (f32[2,15]{1,0:T(2,128)S(1)}, f32[2,15]{1,0:T(2,128)S(1)}, u32[]{:S(2)}, u32[]{:S(2)}) collective-permute-start(f32[2,15]{1,0:T(2,128)S(1)} %constant_dynamic-slice_fusion), channel_id=1, source_target_pairs={{0,1},{1,0},{2,3},{3,2},{4,5},{5,4},{6,7},{7,6},{8,9},{9,8},{10,11... | collective-permute-start | bytes 368 | tf_op jit(solution)/shard_map/ppermute | solution.py:179
  711.5 23.9 %collective-permute-start.32 = (bf16[256,1920]{1,0:T(8,128)(2,1)}, bf16[256,1920]{1,0:T(8,128)(2,1)S(1)}, u32[]{:S(2)}, u32[]{:S(2)}) collective-permute-start(bf16[256,1920]{1,0:T(8,128)(2,1)} %constant_dynamic-update-slice_fusion.7), channel_id=1, source_target_pairs={{0,2},{2,4},{4,6},{6,0},{1,3},{3,5},{5,7},{7,1},{8,10},{10,12},{12... | collective-permute-start | bytes 2949128 | tf_op jit(solution)/shard_map/ppermute | solution.py:22
  712.0 23.5 %collective-permute-start.31 = (bf16[256,1920]{1,0:T(8,128)(2,1)}, bf16[256,1920]{1,0:T(8,128)(2,1)S(1)}, u32[]{:S(2)}, u32[]{:S(2)}) collective-permute-start(bf16[256,1920]{1,0:T(8,128)(2,1)} %constant_dynamic-update-slice_fusion.7), channel_id=1, source_target_pairs={{0,6},{2,0},{4,2},{6,4},{1,7},{3,1},{5,3},{7,5},{8,14},{10,8},{12,... | collective-permute-start | bytes 2949128 | tf_op jit(solution)/shard_map/ppermute | solution.py:26
  717.7 23.5 %collective-permute-start.16 = (bf16[256,1920]{1,0:T(8,128)(2,1)}, bf16[256,1920]{1,0:T(8,128)(2,1)S(1)}, u32[]{:S(2)}, u32[]{:S(2)}) collective-permute-start(bf16[256,1920]{1,0:T(8,128)(2,1)} %constant_dynamic-update-slice_fusion), channel_id=1, source_target_pairs={{0,8},{8,16},{16,24},{24,0},{1,9},{9,17},{17,25},{25,1},{2,10},{10... | collective-permute-start | bytes 2949128 | tf_op jit(solution)/shard_map/ppermute | solution.py:22
  718.4 23.6 %collective-permute-start.15 = (bf16[256,1920]{1,0:T(8,128)(2,1)}, bf16[256,1920]{1,0:T(8,128)(2,1)S(1)}, u32[]{:S(2)}, u32[]{:S(2)}) collective-permute-start(bf16[256,1920]{1,0:T(8,128)(2,1)} %constant_dynamic-update-slice_fusion), channel_id=1, source_target_pairs={{0,24},{8,0},{16,8},{24,16},{1,25},{9,1},{17,9},{25,17},{2,26},{10... | collective-permute-start | bytes 2949128 | tf_op jit(solution)/shard_map/ppermute | solution.py:26
  735.5 20.1 %collective-permute-start.33 = (bf16[128,1920]{1,0:T(8,128)(2,1)S(1)}, bf16[128,1920]{1,0:T(8,128)(2,1)S(1)}, u32[]{:S(2)}, u32[]{:S(2)}) collective-permute-start(bf16[128,1920]{1,0:T(8,128)(2,1)S(1)} %slice.422), channel_id=1, source_target_pairs={{0,2},{2,4},{4,6},{6,0},{1,3},{3,5},{5,7},{7,1},{8,10},{10,12},{12... | collective-permute-start | bytes 1474568 | tf_op jit(solution)/shard_map/ppermute | solution.py:22
  735.6 20.0 %collective-permute-start.34 = (bf16[128,1920]{1,0:T(8,128)(2,1)S(1)}, bf16[128,1920]{1,0:T(8,128)(2,1)S(1)}, u32[]{:S(2)}, u32[]{:S(2)}) collective-permute-start(bf16[128,1920]{1,0:T(8,128)(2,1)S(1)} %slice.423), channel_id=1, source_target_pairs={{0,6},{2,0},{4,2},{6,4},{1,7},{3,1},{5,3},{7,5},{8,14},{10,8},{12,... | collective-permute-start | bytes 1474568 | tf_op jit(solution)/shard_map/ppermute | solution.py:26
  742.1 18.4 %collective-permute-start.17 = (bf16[128,1920]{1,0:T(8,128)(2,1)}, bf16[128,1920]{1,0:T(8,128)(2,1)}, u32[]{:S(2)}, u32[]{:S(2)}) collective-permute-start(bf16[128,1920]{1,0:T(8,128)(2,1)} %slice.394), channel_id=1, source_target_pairs={{0,8},{8,16},{16,24},{24,0},{1,9},{9,17},{17,25},{25,1},{2,10},{10... | collective-permute-start | bytes 1474568 | tf_op jit(solution)/shard_map/ppermute | solution.py:22
  742.9 18.7 %collective-permute-start.18 = (bf16[128,1920]{1,0:T(8,128)(2,1)}, bf16[128,1920]{1,0:T(8,128)(2,1)}, u32[]{:S(2)}, u32[]{:S(2)}) collective-permute-start(bf16[128,1920]{1,0:T(8,128)(2,1)} %slice.395), channel_id=1, source_target_pairs={{0,24},{8,0},{16,8},{24,16},{1,25},{9,1},{17,9},{25,17},{2,26},{10... | collective-permute-start | bytes 1474568 | tf_op jit(solution)/shard_map/ppermute | solution.py:26
  771.7 16.7 %collective-permute-start.35 = (bf16[4,4,64,375]{3,2,1,0:T(8,128)(2,1)}, bf16[4,4,64,375]{3,2,1,0:T(8,128)(2,1)}, u32[]{:S(2)}, u32[]{:S(2)}) collective-permute-start(bf16[4,4,64,375]{3,2,1,0:T(8,128)(2,1)} %fusion.32), channel_id=1, source_target_pairs={{0,1},{1,0},{2,3},{3,2},{4,5},{5,4},{6,7},{7,6},{8,9},{9,8},{10,11... | collective-permute-start | bytes 2304008 | tf_op jit(solution)/shard_map/ppermute | solution.py:192
  (63 other events, 370.5 us)
Sparse Core Ops, SparseCore 0:
  73.5 280.9 all-reduce.3
